TPU v7x, 512 devices: a whole 4x4x16 slice. The times are simulated.
512 devices in a mesh: blk: 32 (over z_lo, x), grp: 16 (over z_hi, y, core).
Axes of the slice: x: 4, y: 4, z: 16 (z_hi: 2, z_lo: 8; z = z_hi * 8 + z_lo), core: 2. Of those that a mesh axis runs over, the one named last changes fastest.
Arguments:
- positions: float32 [3, 32768], P(None, ('blk', 'grp')), may hold values from -0.25 to 31.25, as said below
- moments: float32 [2, 2, 3, 32768], P(None, None, None, ('blk', 'grp')), may hold values from -6 to 6
- inv_polar_re: float32 [32768], P(('blk', 'grp')), may hold values from 0.5 to 2
- inv_polar_im: float32 [32768], P(('blk', 'grp')), may hold values from -0.5 to 0.5
- mode_field: float32 [2, 3, 32768, 512], P(None, None, ('blk', 'grp')), may hold values from -0.0390625 to 0.0390625
- mode_detune: float32 [512], replicated, may hold values from -1 to 1
- mode_width: float32 [512], replicated, may hold values from 0.05 to 1
Outputs:
- response: float32 [2, 2, 3, 32768], P(None, None, None, ('blk', 'grp'))
Inputs may be any that keep to these rules, and one draw needn't show every extreme that they name: `positions`: dipole n lies within 0.25, in each coordinate, of the lattice site (n % 32, (n // 32) % 32, n // 1024); distinct dipoles are at least 0.5 apart.
All inputs are finite; a program needn't handle non-finite values.
Results may differ from a plain program's by a relative error of at most 0.0003.
Values sent between devices are 32-bit elements; how exact they have to be, the bound alone decides.
A program may use at most 64 MiB of HBM per device.

v0:
```python
import math
import jax
import jax.numpy as jnp
from jax import lax
from jax.sharding import Mesh
from jax.sharding import PartitionSpec as P

BLK_GRP = ("blk_0", "blk_1", "grp_0", "grp_1", "grp_2")
GRP = ("grp_0", "grp_1", "grp_2")
BLK = ("blk_0", "blk_1")
wavenumber = 1.0
coupling = 0.05
near_limit = 0.04


def over_axes(value, axes):
    for axis in axes:
        value = lax.psum(value, axis)
    return value


def laid_out(tiles, dim):
    tiles = jnp.moveaxis(tiles, 0, dim)
    shape = tiles.shape
    return tiles.reshape(*shape[:dim], shape[dim] * shape[dim + 1], *shape[dim + 2 :])


def gather_in_order(value, axes, sequence):
    tiles = value[None]
    for k in sequence:
        tiles = lax.all_gather(tiles, axes[k], axis=0, tiled=True)
    block = [lax.axis_size(axes[k]) for k in reversed(sequence)]
    tiles = tiles.reshape(*block, *value.shape)
    turned = sorted(range(len(sequence)), key=lambda place: sequence[len(sequence) - 1 - place])
    return tiles.transpose(*turned, *range(len(sequence), tiles.ndim)).reshape(-1, *value.shape)


def whole_of(value, axes, sequence, dim):
    return laid_out(gather_in_order(value, axes, sequence), dim)


def sent_to_all(value, axis):
    devices = lax.axis_size(axis)
    return lax.all_to_all(
        jnp.broadcast_to(value[None], (devices, *value.shape)), axis, 0, 0, tiled=True
    )


def gather_directly(value, axis, dim):
    return laid_out(sent_to_all(value, axis), dim)


def sent_together(arrays, axis, dim, along):
    ends, at = ([], 0)
    for a in arrays[:-1]:
        at += a.shape[along]
        ends.append(at)
    both = jnp.concatenate(arrays, axis=along)
    return tuple(jnp.split(gather_directly(both, axis, dim), ends, axis=along))


def cut_along(value, dim, devices):
    before, after = (value.shape[:dim], value.shape[dim + 1 :])
    return jnp.moveaxis(value.reshape(*before, devices, -1, *after), dim, 0)


def sent_and_summed(value, axis, dim):
    tiles = cut_along(value, dim, lax.axis_size(axis))
    arrived = lax.all_to_all(tiles, axis, split_axis=0, concat_axis=0, tiled=True)
    return arrived.sum(axis=0)


def pair_field(deltas, dipoles, axis_sum):
    delta_x, delta_y, delta_z = deltas
    square = delta_x * delta_x + delta_y * delta_y + delta_z * delta_z
    coincide = square < near_limit
    safe_square = jnp.where(coincide, 1.0, square)
    inverse = 1.0 / jnp.sqrt(safe_square)
    phase_arg = wavenumber * safe_square * inverse
    cos_val = jnp.cos(phase_arg)
    sine_val = jnp.sin(phase_arg)
    masked_cube = jnp.where(coincide, 0.0, inverse * inverse * inverse)
    near_re = phase_arg * phase_arg - 1.0
    far_re = 3.0 - phase_arg * phase_arg
    diag_re = (cos_val * near_re - sine_val * phase_arg) * masked_cube
    diag_im = (sine_val * near_re + cos_val * phase_arg) * masked_cube
    scaled = masked_cube / safe_square
    outer_re = (cos_val * far_re + 3.0 * sine_val * phase_arg) * scaled
    outer_im = (sine_val * far_re - 3.0 * cos_val * phase_arg) * scaled
    tile_list = []
    for drive_set in range(len(dipoles) // 6):
        moment_re = dipoles[6 * drive_set : 6 * drive_set + 3]
        moment_im = dipoles[6 * drive_set + 3 : 6 * drive_set + 6]
        proj_re = delta_x * moment_re[0] + delta_y * moment_re[1] + delta_z * moment_re[2]
        proj_im = delta_x * moment_im[0] + delta_y * moment_im[1] + delta_z * moment_im[2]
        along_re = outer_re * proj_re - outer_im * proj_im
        along_im = outer_re * proj_im + outer_im * proj_re
        for component in range(3):
            tile_list.append(
                diag_re * moment_re[component]
                - diag_im * moment_im[component]
                + deltas[component] * along_re
            )
        for component in range(3):
            tile_list.append(
                diag_re * moment_im[component]
                + diag_im * moment_re[component]
                + deltas[component] * along_im
            )
    return jnp.stack([jnp.sum(entry_tile, axis=axis_sum) for entry_tile in tile_list])


def contract(left, right):
    return lax.dot_general(left, right, (((0,), (1,)), ((), ())), precision=lax.Precision.HIGHEST)


def modal_project(mode_rows, moment_rows):
    amp_re = contract(mode_rows[0], moment_rows[:, 0]) - contract(mode_rows[1], moment_rows[:, 1])
    amp_im = contract(mode_rows[0], moment_rows[:, 1]) + contract(mode_rows[1], moment_rows[:, 0])
    return (amp_re, amp_im)


def spread(weights, rows):
    return lax.dot_general(weights, rows, (((0,), (1,)), ((), ())), precision=lax.Precision.HIGHEST)


def modal_spread(mode_rows, amp_re, amp_im, mode_detune, mode_width):
    denominator = mode_detune * mode_detune + mode_width * mode_width
    resp_re = (mode_detune / denominator)[:, None]
    resp_im = (mode_width / denominator)[:, None]
    weighted_re = resp_re * amp_re - resp_im * amp_im
    weighted_im = resp_re * amp_im + resp_im * amp_re
    out_re = spread(weighted_re, mode_rows[0]) - spread(weighted_im, mode_rows[1])
    out_im = spread(weighted_re, mode_rows[1]) + spread(weighted_im, mode_rows[0])
    return jnp.stack([out_re, out_im], axis=1)


def combine(moments, inv_polar_re, inv_polar_im, pair_part, modal_part):
    drives = moments.shape[0]
    dipole_count = moments.shape[3]
    field_sum = coupling * pair_part.reshape(drives, 2, 3, dipole_count) + modal_part.reshape(
        drives, 2, 3, dipole_count
    )
    moment_re = moments[:, 0]
    moment_im = moments[:, 1]
    resp_re = inv_polar_re * moment_re - inv_polar_im * moment_im - field_sum[:, 0]
    resp_im = inv_polar_re * moment_im + inv_polar_im * moment_re - field_sum[:, 1]
    return jnp.stack([resp_re, resp_im], axis=1)


def on_device(positions, moments, inv_polar_re, inv_polar_im, mode_field, mode_detune, mode_width):
    drives = moments.shape[0]
    dipole_count = positions.shape[1]
    flat_moments = moments.reshape(drives * 6, dipole_count)
    mode_rows = mode_field.reshape(2, 3 * dipole_count, mode_field.shape[3])
    amp_re, amp_im = modal_project(mode_rows, moments.reshape(drives, 2, 3 * dipole_count))
    amp_re, amp_im = (over_axes(amp_re, BLK_GRP), over_axes(amp_im, BLK_GRP))
    modal_part = modal_spread(mode_rows, amp_re, amp_im, mode_detune, mode_width).reshape(
        drives * 6, dipole_count
    )
    group_pos = whole_of(positions, (("grp_0", "grp_1"), "grp_2"), (0, 1), 1)
    initial = jnp.zeros((drives * 6, group_pos.shape[1]), jnp.float32)
    places, dipoles = sent_together((positions, flat_moments), BLK, 1, 0)
    columns = places.shape[1]
    block_width = math.gcd(columns, 256)

    def advance(block, inner):
        source_pos = lax.dynamic_slice_in_dim(places, block * block_width, block_width, 1)
        source_mom = lax.dynamic_slice_in_dim(dipoles, block * block_width, block_width, 1)
        deltas = [group_pos[axis_c][None, :] - source_pos[axis_c][:, None] for axis_c in range(3)]
        return inner + pair_field(
            deltas, [source_mom[member][:, None] for member in range(drives * 6)], 0
        )

    partial_value = lax.fori_loop(0, columns // block_width, advance, initial)
    pair_part = sent_and_summed(partial_value, GRP, 1)
    return combine(moments, inv_polar_re, inv_polar_im, pair_part, modal_part)


def solution(mesh):
    torus = Mesh(mesh.devices.reshape(8, 4, 2, 4, 2), ("blk_0", "blk_1", "grp_0", "grp_1", "grp_2"))
    placed = (
        P(None, BLK_GRP),
        P(None, None, None, BLK_GRP),
        P(BLK_GRP),
        P(BLK_GRP),
        P(None, None, BLK_GRP, None),
        P(),
        P(),
    )
    return jax.shard_map(
        on_device,
        mesh=torus,
        in_specs=placed,
        out_specs=P(None, None, None, BLK_GRP),
        check_vma=False,
    )
```

profile of v0, /device:TPU:1, one launch (start us, length us, event | category | flops | bytes accessed | tf_op | source)
XLA Modules:
  0.0 260.5 jit_solution(8766813554993038770)
XLA Ops:
  0.0 0.8 copy.39
  0.8 0.7 pad_maximum_fusion
  1.5 0.8 reshape.63
  2.3 15.9 %all-to-all-start = ((f32[32,1,960]{2,1,0:T(1,128)}), f32[32,1,960]{2,1,0:T(1,128)S(1)}, u32[]{:S(2)}, u32[]{:S(2)}) async-start(f32[32,1,960]{2,1,0:T(1,128)} %reshape.63), calls=%async_computation | async-start | bytes 262144 | tf_op jit(solution)/shard_map/all_to_all | solution.py:44
  18.3 0.1 reshape.58
  18.3 0.1 fusion.64
  18.4 0.3 fusion.49
  18.8 0.3 fusion.53
  19.1 0.3 convolution_add_fusion
  19.4 0.3 convolution_subtract_fusion
  19.7 29.8 %all-reduce = (f32[512,2]{0,1:T(2,128)S(1)}, f32[512,2]{0,1:T(2,128)S(1)}) all-reduce(f32[512,2]{0,1:T(2,128)S(1)} %convolution_add_fusion, f32[512,2]{0,1:T(2,128)S(1)} %convolution_subtract_fusion), channel_id=1, replica_groups=mesh['blk_0'=8,'blk_1'=4,'grp_0'=2,'grp_1'=4,'grp_2'=2] {'blk_0'}, use_global_device_ids=true, to_apply=%region_20.0 | all-reduce | flops 2048 | bytes 16384 | tf_op jit(solution)/shard_map/psum | solution.py:18
  49.5 8.5 %all-reduce.2 = (f32[512,2]{0,1:T(2,128)S(1)}, f32[512,2]{0,1:T(2,128)S(1)}) all-reduce(f32[512,2]{0,1:T(2,128)S(1)} %get-tuple-element.184, f32[512,2]{0,1:T(2,128)S(1)} %get-tuple-element.185), channel_id=1, replica_groups=mesh['blk_0'=8,'blk_1'=4,'grp_0'=2,'grp_1'=4,'grp_2'=2] {'blk_1'}, use_global_device_ids=true, to_apply=%region_21.0 | all-reduce | flops 2048 | bytes 16384 | tf_op jit(solution)/shard_map/psum | solution.py:18
  58.1 12.6 %all-reduce.4 = (f32[512,2]{0,1:T(2,128)S(1)}, f32[512,2]{0,1:T(2,128)S(1)}) all-reduce(f32[512,2]{0,1:T(2,128)S(1)} %get-tuple-element.188, f32[512,2]{0,1:T(2,128)S(1)} %get-tuple-element.189), channel_id=1, replica_groups=mesh['blk_0'=8,'blk_1'=4,'grp_0'=2,'grp_1'=4,'grp_2'=2] {'grp_0'}, use_global_device_ids=true, to_apply=%region_22.0 | all-reduce | flops 2048 | bytes 16384 | tf_op jit(solution)/shard_map/psum | solution.py:18
  70.6 9.1 %all-reduce.1 = (f32[512,2]{0,1:T(2,128)S(1)}, f32[512,2]{0,1:T(2,128)S(1)}) all-reduce(f32[512,2]{0,1:T(2,128)S(1)} %get-tuple-element.192, f32[512,2]{0,1:T(2,128)S(1)} %get-tuple-element.193), channel_id=1, replica_groups=mesh['blk_0'=8,'blk_1'=4,'grp_0'=2,'grp_1'=4,'grp_2'=2] {'grp_1'}, use_global_device_ids=true, to_apply=%region_23.24 | all-reduce | flops 2048 | bytes 16384 | tf_op jit(solution)/shard_map/psum | solution.py:18
  79.8 12.2 %all-reduce.3 = (f32[512,2]{0,1:T(2,128)S(1)}, f32[512,2]{0,1:T(2,128)S(1)}) all-reduce(f32[512,2]{0,1:T(2,128)S(1)} %get-tuple-element.186, f32[512,2]{0,1:T(2,128)S(1)} %get-tuple-element.187), channel_id=1, replica_groups=mesh['blk_0'=8,'blk_1'=4,'grp_0'=2,'grp_1'=4,'grp_2'=2] {'grp_2'}, use_global_device_ids=true, to_apply=%region_24.25 | all-reduce | flops 2048 | bytes 16384 | tf_op jit(solution)/shard_map/psum | solution.py:18
  92.0 0.4 fusion.62
  92.4 0.4 convolution_subtract_fusion.1
  92.9 0.1 stack.144
  93.0 0.2 copy-done.1
  93.1 53.9 %all-gather.1 = f32[8,3,64]{2,1,0:T(4,128)S(1)} all-gather(f32[1,3,64]{2,1,0:T(4,128)S(1)} %bitcast.166), channel_id=2, replica_groups=mesh['blk_0'=8,'blk_1'=4,'grp_0'=2,'grp_1'=4,'grp_2'=2] {'grp_0','grp_1'}, dimensions={0}, use_global_device_ids=true | all-gather | bytes 6912 | tf_op jit(solution)/shard_map/all_gather | solution.py:31
  147.0 6.4 %all_gather.7 = f32[16,3,64]{2,0,1:T(8,128)S(1)} all-gather(f32[8,3,64]{2,0,1:T(8,128)S(1)} %copy.41), channel_id=1, replica_groups=mesh['blk_0'=8,'blk_1'=4,'grp_0'=2,'grp_1'=4,'grp_2'=2] {'grp_2'}, dimensions={0}, use_global_device_ids=true | all-gather | bytes 18432 | tf_op jit(solution)/shard_map/all_gather | solution.py:31
  153.5 0.1 reshape.55
  153.6 0.4 fusion.61
  154.0 0.6 broadcast.270
  154.6 0.9 reduce
  155.5 0.1 reshape.64
  155.7 0.1 copy.45
  155.7 0.1 split.13
  155.8 0.1 split.11
  155.9 79.1 %while.16 = (s32[]{:T(128)}, f32[12,1024]{1,0:T(8,128)S(1)}, f32[3,1024]{1,0:T(4,128)S(1)}, f32[3,2048]{1,0:T(4,128)S(1)}, f32[12,2048]{1,0:T(8,128)S(1)}, /*ind...) while((s32[]{:T(128)}, f32[12,1024]{1,0:T(8,128)S(1)}, ...), condition=%wide.region_13.0_spmd.clone, body=%wide.region_0.13_spmd.clone.sunk | while | flops 36712464 | bytes 378273 | solution.py:175
  156.0 0.1 constant_dynamic-slice_fusion.3
  156.1 9.6 %fusion.77 = (f32[1024]{0:T(1024)S(1)}, f32[1024]{0:T(1024)S(1)}, f32[1024]{0:T(1024)S(1)}, f32[1024]{0:T(1024)S(1)}, f32[1024]{0:T(1024)S(1)}, /*index=5*/f32[1...) fusion(f32[256]{0:T(256)S(1)} %bitcast.160, ...), kind=kLoop, calls=%fused_computation.76.clone.1 | loop fusion | flops 36687872 | bytes 76800 | tf_op jit(solution)/shard_map/while/body/eval_jaxpr/reduce_sum | solution.py:110
  165.7 0.1 stack.162
  165.8 0.1 constant_dynamic-slice_fusion.3
  166.0 9.6 %fusion.77 = (f32[1024]{0:T(1024)S(1)}, f32[1024]{0:T(1024)S(1)}, f32[1024]{0:T(1024)S(1)}, f32[1024]{0:T(1024)S(1)}, f32[1024]{0:T(1024)S(1)}, /*index=5*/f32[1...) fusion(f32[256]{0:T(256)S(1)} %bitcast.160, ...), kind=kLoop, calls=%fused_computation.76.clone.1 | loop fusion | flops 36687872 | bytes 76800 | tf_op jit(solution)/shard_map/while/body/eval_jaxpr/reduce_sum | solution.py:110
  175.6 0.1 stack.162
  175.7 0.1 constant_dynamic-slice_fusion.3
  175.9 9.6 %fusion.77 = (f32[1024]{0:T(1024)S(1)}, f32[1024]{0:T(1024)S(1)}, f32[1024]{0:T(1024)S(1)}, f32[1024]{0:T(1024)S(1)}, f32[1024]{0:T(1024)S(1)}, /*index=5*/f32[1...) fusion(f32[256]{0:T(256)S(1)} %bitcast.160, ...), kind=kLoop, calls=%fused_computation.76.clone.1 | loop fusion | flops 36687872 | bytes 76800 | tf_op jit(solution)/shard_map/while/body/eval_jaxpr/reduce_sum | solution.py:110
  185.5 0.1 stack.162
  185.6 0.1 constant_dynamic-slice_fusion.3
  185.8 9.6 %fusion.77 = (f32[1024]{0:T(1024)S(1)}, f32[1024]{0:T(1024)S(1)}, f32[1024]{0:T(1024)S(1)}, f32[1024]{0:T(1024)S(1)}, f32[1024]{0:T(1024)S(1)}, /*index=5*/f32[1...) fusion(f32[256]{0:T(256)S(1)} %bitcast.160, ...), kind=kLoop, calls=%fused_computation.76.clone.1 | loop fusion | flops 36687872 | bytes 76800 | tf_op jit(solution)/shard_map/while/body/eval_jaxpr/reduce_sum | solution.py:110
  195.3 0.1 stack.162
  195.5 0.1 constant_dynamic-slice_fusion.3
  195.6 9.6 %fusion.77 = (f32[1024]{0:T(1024)S(1)}, f32[1024]{0:T(1024)S(1)}, f32[1024]{0:T(1024)S(1)}, f32[1024]{0:T(1024)S(1)}, f32[1024]{0:T(1024)S(1)}, /*index=5*/f32[1...) fusion(f32[256]{0:T(256)S(1)} %bitcast.160, ...), kind=kLoop, calls=%fused_computation.76.clone.1 | loop fusion | flops 36687872 | bytes 76800 | tf_op jit(solution)/shard_map/while/body/eval_jaxpr/reduce_sum | solution.py:110
  205.2 0.1 stack.162
  205.4 0.1 constant_dynamic-slice_fusion.3
  205.5 9.6 %fusion.77 = (f32[1024]{0:T(1024)S(1)}, f32[1024]{0:T(1024)S(1)}, f32[1024]{0:T(1024)S(1)}, f32[1024]{0:T(1024)S(1)}, f32[1024]{0:T(1024)S(1)}, /*index=5*/f32[1...) fusion(f32[256]{0:T(256)S(1)} %bitcast.160, ...), kind=kLoop, calls=%fused_computation.76.clone.1 | loop fusion | flops 36687872 | bytes 76800 | tf_op jit(solution)/shard_map/while/body/eval_jaxpr/reduce_sum | solution.py:110
  215.1 0.1 stack.162
  215.3 0.1 constant_dynamic-slice_fusion.3
  215.4 9.6 %fusion.77 = (f32[1024]{0:T(1024)S(1)}, f32[1024]{0:T(1024)S(1)}, f32[1024]{0:T(1024)S(1)}, f32[1024]{0:T(1024)S(1)}, f32[1024]{0:T(1024)S(1)}, /*index=5*/f32[1...) fusion(f32[256]{0:T(256)S(1)} %bitcast.160, ...), kind=kLoop, calls=%fused_computation.76.clone.1 | loop fusion | flops 36687872 | bytes 76800 | tf_op jit(solution)/shard_map/while/body/eval_jaxpr/reduce_sum | solution.py:110
  225.0 0.1 stack.162
  225.1 0.1 constant_dynamic-slice_fusion.3
  225.3 9.6 %fusion.77 = (f32[1024]{0:T(1024)S(1)}, f32[1024]{0:T(1024)S(1)}, f32[1024]{0:T(1024)S(1)}, f32[1024]{0:T(1024)S(1)}, f32[1024]{0:T(1024)S(1)}, /*index=5*/f32[1...) fusion(f32[256]{0:T(256)S(1)} %bitcast.160, ...), kind=kLoop, calls=%fused_computation.76.clone.1 | loop fusion | flops 36687872 | bytes 76800 | tf_op jit(solution)/shard_map/while/body/eval_jaxpr/reduce_sum | solution.py:110
  234.9 0.1 stack.162
  235.0 0.1 reshape.57
  235.1 0.7 reshape.65
  235.9 7.9 %all-to-all-start.1 = ((f32[16,1,768]{2,1,0:T(1,128)}), f32[16,1,768]{2,1,0:T(1,128)S(1)}, u32[]{:S(2)}, u32[]{:S(2)}) async-start(f32[16,1,768]{2,1,0:T(1,128)} %reshape.65), calls=%async_computation.1 | async-start | bytes 98304 | tf_op jit(solution)/shard_map/all_to_all | solution.py:69
  243.8 0.4 convolution_add_fusion.1
  244.2 0.1 stack.145
  244.3 14.0 %all-to-all-done.1 = f32[16,1,768]{2,1,0:T(1,128)S(1)} async-done(((f32[16,1,768]{2,1,0:T(1,128)}), f32[16,1,768]{2,1,0:T(1,128)S(1)}, u32[]{:S(2)}, u32[]{:S(2)}) %all-to-all-start.1) | async-done | bytes 49184 | tf_op jit(solution)/shard_map/all_to_all | solution.py:69
  258.3 0.7 reduce.1
  259.1 0.1 reshape.66
  259.3 0.6 copy-done.4
  259.9 0.6 copy.50
  (44 shorter events, 0.5 us)
Async XLA Ops:
  0.0 18.3 %copy-start = (f32[2,3,64,512]{3,2,1,0:T(8,128)S(1)}, f32[2,3,64,512]{3,2,1,0:T(8,128)}, u32[]{:S(2)}) copy-start(f32[2,3,64,512]{3,2,1,0:T(8,128)} %param.13) | copy-start | bytes 2359300
  2.3 151.6 %all-to-all-start = ((f32[32,1,960]{2,1,0:T(1,128)}), f32[32,1,960]{2,1,0:T(1,128)S(1)}, u32[]{:S(2)}, u32[]{:S(2)}) async-start(f32[32,1,960]{2,1,0:T(1,128)} %reshape.63), calls=%async_computation | async-start | bytes 262144 | tf_op jit(solution)/shard_map/all_to_all | solution.py:44
  79.8 12.2 %copy-start.2 = (f32[512]{0:T(512)S(1)}, f32[512]{0:T(512)}, u32[]{:S(2)}) copy-start(f32[512]{0:T(512)} %param.14) | copy-start | bytes 6148
  79.8 12.2 %copy-start.3 = (f32[512]{0:T(512)S(1)}, f32[512]{0:T(512)}, u32[]{:S(2)}) copy-start(f32[512]{0:T(512)} %param.15) | copy-start | bytes 6148
  92.4 0.7 copy-start.1
  235.9 22.5 %all-to-all-start.1 = ((f32[16,1,768]{2,1,0:T(1,128)}), f32[16,1,768]{2,1,0:T(1,128)S(1)}, u32[]{:S(2)}, u32[]{:S(2)}) async-start(f32[16,1,768]{2,1,0:T(1,128)} %reshape.65), calls=%async_computation.1 | async-start | bytes 98304 | tf_op jit(solution)/shard_map/all_to_all | solution.py:69
  259.2 0.7 copy-start.4
  259.3 0.7 copy-start.5
where the time goes:
time: 261 us
  blocking collectives  133 us (51%)
  other arithmetic  79.1 us (30%)
  starting transfers between devices  23.9 us (9%)
  waiting for transfers between devices  14 us (5%)
  local copies, waits for them, and re-layouts  7.4 us (3%)
  matrix products  2.91 us (1%)
    reduce_sum x8, other arithmetic, pair_field(): jnp.sum(entry_tile, axis=axis_sum)  76.6 us
    psum x5, blocking collectives, over_axes(): value = lax.psum(value, axis)  72.2 us
    all_gather x2, blocking collectives, gather_in_order(): tiles = lax.all_gather(tiles, axes[k], axis=0, tiled=True)  60.3 us
    all_to_all x1, starting transfers between devices, sent_to_all(): lax.all_to_all(jnp.broadcast_to(value[None], (devices, *value.shape)), ax...  15.9 us
    all_to_all x1, waiting for transfers between devices, sent_and_summed(): lax.all_to_all(tiles, axis, split_axis=0, concat_axis=0, tiled=True)  14 us
    all_to_all x1, starting transfers between devices, sent_and_summed(): lax.all_to_all(tiles, axis, split_axis=0, concat_axis=0, tiled=True)  7.95 us
  transfers between devices with their start and end apart: 2, of which 1 were waited for; matrix products, arithmetic and copies ran while one was open for 1% of the time, Pallas kernels for 0%

commit v1 on v0

--- a/solution.py
+++ b/solution.py
@@ -28,7 +28,9 @@
 def gather_in_order(value, axes, sequence):
     tiles = value[None]
     for k in sequence:
-        tiles = lax.all_gather(tiles, axes[k], axis=0, tiled=True)
+        tiles = jnp.concatenate(
+            lax.all_to_all(jnp.stack([tiles] * lax.axis_size(axes[k])), axes[k], 0, 0), axis=0
+        )
     block = [lax.axis_size(axes[k]) for k in reversed(sequence)]
     tiles = tiles.reshape(*block, *value.shape)
     turned = sorted(range(len(sequence)), key=lambda place: sequence[len(sequence) - 1 - place])

time: 261 us -> 227 us (0.87)
  blocking collectives: 133 us -> 71.3 us
  starting transfers between devices: 23.9 us -> 36.7 us
  waiting for transfers between devices: 14 us -> 24.3 us
    all_gather x2 -> x0, blocking collectives: 60.3 us -> none  [gather_in_order(): tiles = lax.all_gather(tiles, axes[k], axis=0, tiled=True)]
    all_to_all x0 -> x1, starting transfers between devices: none -> 18.4 us  [gather_in_order(): lax.all_to_all(jnp.stack([tiles] * lax.axis_size(axes[k])), axes[k], 0, 0)]
    all_to_all x1, starting transfers between devices: 15.9 us -> 3.85 us  [sent_to_all(): lax.all_to_all(jnp.broadcast_to(value[None], (devices, *value.shape)), ax...]
    all_to_all x1, waiting for transfers between devices: 0.01 us -> 10.3 us  [sent_to_all(): lax.all_to_all(jnp.broadcast_to(value[None], (devices, *value.shape)), ax...]
    all_to_all x1, starting transfers between devices: 7.95 us -> 14.5 us  [sent_and_summed(): lax.all_to_all(tiles, axis, split_axis=0, concat_axis=0, tiled=True)]
    psum x5, blocking collectives: 72.2 us -> 67.6 us  [over_axes(): value = lax.psum(value, axis)]
    all_to_all x0 -> x1, blocking collectives: none -> 3.72 us  [gather_in_order(): lax.all_to_all(jnp.stack([tiles] * lax.axis_size(axes[k])), axes[k], 0, 0)]
  transfers between devices with their start and end apart: 2 -> 3, of which waited for: 1 -> 2; matrix products, arithmetic and copies ran while one was open for 1% -> 3% of each run, Pallas kernels for 0% -> 0%
where the time goes in v1:
time: 227 us; the launch traced here: 226 us
  other arithmetic  80.7 us (36%)
  blocking collectives  71.3 us (31%)
  starting transfers between devices  36.7 us (16%)
  waiting for transfers between devices  24.3 us (11%)
  local copies, waits for them, and re-layouts  9.43 us (4%)
  matrix products  2.89 us (1%)
    reduce_sum x8, other arithmetic, pair_field(): jnp.sum(entry_tile, axis=axis_sum)  76.6 us
    psum x5, blocking collectives, over_axes(): value = lax.psum(value, axis)  67.6 us
    all_to_all x1, starting transfers between devices, gather_in_order(): lax.all_to_all(jnp.stack([tiles] * lax.axis_size(axes[k])), axes[k], 0, 0)  18.4 us
    all_to_all x1, starting transfers between devices, sent_and_summed(): lax.all_to_all(tiles, axis, split_axis=0, concat_axis=0, tiled=True)  14.5 us
    all_to_all x1, waiting for transfers between devices, sent_and_summed(): lax.all_to_all(tiles, axis, split_axis=0, concat_axis=0, tiled=True)  14 us
    all_to_all x1, waiting for transfers between devices, sent_to_all(): lax.all_to_all(jnp.broadcast_to(value[None], (devices, *value.shape)), ax...  10.3 us
    unnamed x23, local copies, waits for them, and re-layouts  4.88 us
  transfers between devices with their start and end apart: 3, of which 2 were waited for; matrix products, arithmetic and copies ran while one was open for 3% of the time, Pallas kernels for 0%

profile of v1, /device:TPU:1, one launch (start us, length us, event | category | flops | bytes accessed | tf_op | source)
XLA Modules:
  0.0 226.1 jit_solution(11723145948368241598)
XLA Ops:
  0.0 0.7 broadcast_bitcast_fusion
  0.7 0.6 broadcast.272
  1.3 0.7 reduce
  2.0 0.7 reshape.57
  2.7 18.4 %all-to-all-start = ((f32[8,1,192]{2,1,0:T(1,128)}), f32[8,1,192]{2,1,0:T(1,128)S(1)}, u32[]{:S(2)}, u32[]{:S(2)}) async-start(f32[8,1,192]{2,1,0:T(1,128)} %reshape.57), calls=%async_computation | async-start | bytes 16384 | tf_op jit(solution)/shard_map/all_to_all | solution.py:32
  21.2 1.2 fusion.64
  22.4 0.3 fusion.49
  22.7 0.3 fusion.53
  23.0 0.3 convolution_add_fusion
  23.3 0.3 convolution_subtract_fusion
  23.7 25.6 %all-reduce = (f32[512,2]{0,1:T(2,128)S(1)}, f32[512,2]{0,1:T(2,128)S(1)}) all-reduce(f32[512,2]{0,1:T(2,128)S(1)} %convolution_add_fusion, f32[512,2]{0,1:T(2,128)S(1)} %convolution_subtract_fusion), channel_id=1, replica_groups=mesh['blk_0'=8,'blk_1'=4,'grp_0'=2,'grp_1'=4,'grp_2'=2] {'blk_0'}, use_global_device_ids=true, to_apply=%region_20.0 | all-reduce | flops 2048 | bytes 16384 | tf_op jit(solution)/shard_map/psum | solution.py:18
  49.3 8.6 %all-reduce.2 = (f32[512,2]{0,1:T(2,128)S(1)}, f32[512,2]{0,1:T(2,128)S(1)}) all-reduce(f32[512,2]{0,1:T(2,128)S(1)} %get-tuple-element.184, f32[512,2]{0,1:T(2,128)S(1)} %get-tuple-element.185), channel_id=1, replica_groups=mesh['blk_0'=8,'blk_1'=4,'grp_0'=2,'grp_1'=4,'grp_2'=2] {'blk_1'}, use_global_device_ids=true, to_apply=%region_21.0 | all-reduce | flops 2048 | bytes 16384 | tf_op jit(solution)/shard_map/psum | solution.py:18
  57.9 12.6 %all-reduce.4 = (f32[512,2]{0,1:T(2,128)S(1)}, f32[512,2]{0,1:T(2,128)S(1)}) all-reduce(f32[512,2]{0,1:T(2,128)S(1)} %get-tuple-element.188, f32[512,2]{0,1:T(2,128)S(1)} %get-tuple-element.189), channel_id=1, replica_groups=mesh['blk_0'=8,'blk_1'=4,'grp_0'=2,'grp_1'=4,'grp_2'=2] {'grp_0'}, use_global_device_ids=true, to_apply=%region_22.0 | all-reduce | flops 2048 | bytes 16384 | tf_op jit(solution)/shard_map/psum | solution.py:18
  70.5 9.1 %all-reduce.1 = (f32[512,2]{0,1:T(2,128)S(1)}, f32[512,2]{0,1:T(2,128)S(1)}) all-reduce(f32[512,2]{0,1:T(2,128)S(1)} %get-tuple-element.192, f32[512,2]{0,1:T(2,128)S(1)} %get-tuple-element.193), channel_id=1, replica_groups=mesh['blk_0'=8,'blk_1'=4,'grp_0'=2,'grp_1'=4,'grp_2'=2] {'grp_1'}, use_global_device_ids=true, to_apply=%region_23.24 | all-reduce | flops 2048 | bytes 16384 | tf_op jit(solution)/shard_map/psum | solution.py:18
  79.6 11.7 %all-reduce.3 = (f32[512,2]{0,1:T(2,128)S(1)}, f32[512,2]{0,1:T(2,128)S(1)}) all-reduce(f32[512,2]{0,1:T(2,128)S(1)} %get-tuple-element.186, f32[512,2]{0,1:T(2,128)S(1)} %get-tuple-element.187), channel_id=1, replica_groups=mesh['blk_0'=8,'blk_1'=4,'grp_0'=2,'grp_1'=4,'grp_2'=2] {'grp_2'}, use_global_device_ids=true, to_apply=%region_24.25 | all-reduce | flops 2048 | bytes 16384 | tf_op jit(solution)/shard_map/psum | solution.py:18
  91.3 0.4 fusion.62
  91.7 0.3 copy-done
  92.0 0.8 reshape.61
  92.9 0.7 reduce.1
  93.7 0.1 reshape.59
  93.8 3.7 %all_to_all.20 = f32[2,1,1536]{2,1,0:T(1,128)S(1)} all-to-all(f32[2,1,1536]{2,1,0:T(1,128)S(1)} %reshape.59), channel_id=1, replica_groups=mesh['blk_0'=8,'blk_1'=4,'grp_0'=2,'grp_1'=4,'grp_2'=2] {'grp_2'}, dimensions={0} | all-to-all | bytes 24576 | tf_op jit(solution)/shard_map/all_to_all | solution.py:32
  97.5 3.9 %all-to-all-start.2 = ((f32[32,1,960]{2,1,0:T(1,128)}), f32[32,1,960]{2,1,0:T(1,128)S(1)}, u32[]{:S(2)}, u32[]{:S(2)}) async-start(f32[32,1,960]{2,1,0:T(1,128)} %reshape.61), calls=%async_computation.2 | async-start | bytes 262144 | tf_op jit(solution)/shard_map/all_to_all | solution.py:46
  101.4 0.4 convolution_subtract_fusion.1
  101.8 0.1 stack.152
  101.9 0.4 fusion.61
  102.3 0.7 reduce.2
  103.3 10.3 %all-to-all-done.2 = f32[32,1,960]{2,1,0:T(1,128)S(1)} async-done(((f32[32,1,960]{2,1,0:T(1,128)}), f32[32,1,960]{2,1,0:T(1,128)S(1)}, u32[]{:S(2)}, u32[]{:S(2)}) %all-to-all-start.2) | async-done | bytes 122912 | tf_op jit(solution)/shard_map/all_to_all | solution.py:46
  113.5 1.0 reduce.3
  114.5 0.1 reshape.62
  114.7 0.1 split.13
  114.9 0.1 split.11
  115.0 79.1 %while.16 = (s32[]{:T(128)}, f32[12,1024]{1,0:T(8,128)S(1)}, f32[3,1024]{1,0:T(4,128)S(1)}, f32[3,2048]{1,0:T(4,128)S(1)}, f32[12,2048]{1,0:T(8,128)S(1)}, /*ind...) while((s32[]{:T(128)}, f32[12,1024]{1,0:T(8,128)S(1)}, ...), condition=%wide.region_13.0_spmd.clone, body=%wide.region_0.13_spmd.clone.sunk | while | flops 36712464 | bytes 378273 | solution.py:177
  115.0 0.1 constant_dynamic-slice_fusion.3
  115.1 9.6 %fusion.77 = (f32[1024]{0:T(1024)S(1)}, f32[1024]{0:T(1024)S(1)}, f32[1024]{0:T(1024)S(1)}, f32[1024]{0:T(1024)S(1)}, f32[1024]{0:T(1024)S(1)}, /*index=5*/f32[1...) fusion(f32[256]{0:T(256)S(1)} %bitcast.169, ...), kind=kLoop, calls=%fused_computation.76.clone.1 | loop fusion | flops 36687872 | bytes 76800 | tf_op jit(solution)/shard_map/while/body/eval_jaxpr/reduce_sum | solution.py:112
  124.7 0.1 stack.171
  124.9 0.1 constant_dynamic-slice_fusion.3
  125.0 9.6 %fusion.77 = (f32[1024]{0:T(1024)S(1)}, f32[1024]{0:T(1024)S(1)}, f32[1024]{0:T(1024)S(1)}, f32[1024]{0:T(1024)S(1)}, f32[1024]{0:T(1024)S(1)}, /*index=5*/f32[1...) fusion(f32[256]{0:T(256)S(1)} %bitcast.169, ...), kind=kLoop, calls=%fused_computation.76.clone.1 | loop fusion | flops 36687872 | bytes 76800 | tf_op jit(solution)/shard_map/while/body/eval_jaxpr/reduce_sum | solution.py:112
  134.6 0.1 stack.171
  134.7 0.1 constant_dynamic-slice_fusion.3
  134.9 9.6 %fusion.77 = (f32[1024]{0:T(1024)S(1)}, f32[1024]{0:T(1024)S(1)}, f32[1024]{0:T(1024)S(1)}, f32[1024]{0:T(1024)S(1)}, f32[1024]{0:T(1024)S(1)}, /*index=5*/f32[1...) fusion(f32[256]{0:T(256)S(1)} %bitcast.169, ...), kind=kLoop, calls=%fused_computation.76.clone.1 | loop fusion | flops 36687872 | bytes 76800 | tf_op jit(solution)/shard_map/while/body/eval_jaxpr/reduce_sum | solution.py:112
  144.5 0.1 stack.171
  144.6 0.1 constant_dynamic-slice_fusion.3
  144.8 9.6 %fusion.77 = (f32[1024]{0:T(1024)S(1)}, f32[1024]{0:T(1024)S(1)}, f32[1024]{0:T(1024)S(1)}, f32[1024]{0:T(1024)S(1)}, f32[1024]{0:T(1024)S(1)}, /*index=5*/f32[1...) fusion(f32[256]{0:T(256)S(1)} %bitcast.169, ...), kind=kLoop, calls=%fused_computation.76.clone.1 | loop fusion | flops 36687872 | bytes 76800 | tf_op jit(solution)/shard_map/while/body/eval_jaxpr/reduce_sum | solution.py:112
  154.4 0.1 stack.171
  154.5 0.1 constant_dynamic-slice_fusion.3
  154.7 9.6 %fusion.77 = (f32[1024]{0:T(1024)S(1)}, f32[1024]{0:T(1024)S(1)}, f32[1024]{0:T(1024)S(1)}, f32[1024]{0:T(1024)S(1)}, f32[1024]{0:T(1024)S(1)}, /*index=5*/f32[1...) fusion(f32[256]{0:T(256)S(1)} %bitcast.169, ...), kind=kLoop, calls=%fused_computation.76.clone.1 | loop fusion | flops 36687872 | bytes 76800 | tf_op jit(solution)/shard_map/while/body/eval_jaxpr/reduce_sum | solution.py:112
  164.2 0.1 stack.171
  164.4 0.1 constant_dynamic-slice_fusion.3
  164.5 9.6 %fusion.77 = (f32[1024]{0:T(1024)S(1)}, f32[1024]{0:T(1024)S(1)}, f32[1024]{0:T(1024)S(1)}, f32[1024]{0:T(1024)S(1)}, f32[1024]{0:T(1024)S(1)}, /*index=5*/f32[1...) fusion(f32[256]{0:T(256)S(1)} %bitcast.169, ...), kind=kLoop, calls=%fused_computation.76.clone.1 | loop fusion | flops 36687872 | bytes 76800 | tf_op jit(solution)/shard_map/while/body/eval_jaxpr/reduce_sum | solution.py:112
  174.1 0.1 stack.171
  174.3 0.1 constant_dynamic-slice_fusion.3
  174.4 9.6 %fusion.77 = (f32[1024]{0:T(1024)S(1)}, f32[1024]{0:T(1024)S(1)}, f32[1024]{0:T(1024)S(1)}, f32[1024]{0:T(1024)S(1)}, f32[1024]{0:T(1024)S(1)}, /*index=5*/f32[1...) fusion(f32[256]{0:T(256)S(1)} %bitcast.169, ...), kind=kLoop, calls=%fused_computation.76.clone.1 | loop fusion | flops 36687872 | bytes 76800 | tf_op jit(solution)/shard_map/while/body/eval_jaxpr/reduce_sum | solution.py:112
  184.0 0.1 stack.171
  184.2 0.1 constant_dynamic-slice_fusion.3
  184.3 9.6 %fusion.77 = (f32[1024]{0:T(1024)S(1)}, f32[1024]{0:T(1024)S(1)}, f32[1024]{0:T(1024)S(1)}, f32[1024]{0:T(1024)S(1)}, f32[1024]{0:T(1024)S(1)}, /*index=5*/f32[1...) fusion(f32[256]{0:T(256)S(1)} %bitcast.169, ...), kind=kLoop, calls=%fused_computation.76.clone.1 | loop fusion | flops 36687872 | bytes 76800 | tf_op jit(solution)/shard_map/while/body/eval_jaxpr/reduce_sum | solution.py:112
  193.9 0.1 stack.171
  194.2 0.7 reshape.63
  194.9 14.5 %all-to-all-start.3 = ((f32[16,1,768]{2,1,0:T(1,128)}), f32[16,1,768]{2,1,0:T(1,128)S(1)}, u32[]{:S(2)}, u32[]{:S(2)}) async-start(f32[16,1,768]{2,1,0:T(1,128)} %reshape.63), calls=%async_computation.3 | async-start | bytes 98304 | tf_op jit(solution)/shard_map/all_to_all | solution.py:71
  209.4 0.4 convolution_add_fusion.1
  209.8 0.1 stack.153
  209.9 14.0 %all-to-all-done.3 = f32[16,1,768]{2,1,0:T(1,128)S(1)} async-done(((f32[16,1,768]{2,1,0:T(1,128)}), f32[16,1,768]{2,1,0:T(1,128)S(1)}, u32[]{:S(2)}, u32[]{:S(2)}) %all-to-all-start.3) | async-done | bytes 49184 | tf_op jit(solution)/shard_map/all_to_all | solution.py:71
  223.9 0.8 reduce.4
  224.9 0.6 copy-done.4
  225.5 0.6 copy.60
  (56 shorter events, 1.1 us)
Async XLA Ops:
  2.7 18.4 %copy-start.1 = (f32[2,2,3,64]{3,1,2,0:T(2,128)S(1)}, f32[2,2,3,64]{3,1,2,0:T(2,128)}, u32[]{:S(2)}) copy-start(f32[2,2,3,64]{3,1,2,0:T(2,128)} %param.10) | copy-start | bytes 9220
  2.7 90.2 %all-to-all-start = ((f32[8,1,192]{2,1,0:T(1,128)}), f32[8,1,192]{2,1,0:T(1,128)S(1)}, u32[]{:S(2)}, u32[]{:S(2)}) async-start(f32[8,1,192]{2,1,0:T(1,128)} %reshape.57), calls=%async_computation | async-start | bytes 16384 | tf_op jit(solution)/shard_map/all_to_all | solution.py:32
  79.6 11.7 %copy-start.2 = (f32[512]{0:T(512)S(1)}, f32[512]{0:T(512)}, u32[]{:S(2)}) copy-start(f32[512]{0:T(512)} %param.14) | copy-start | bytes 6148
  79.6 11.7 %copy-start.3 = (f32[512]{0:T(512)S(1)}, f32[512]{0:T(512)}, u32[]{:S(2)}) copy-start(f32[512]{0:T(512)} %param.15) | copy-start | bytes 6148
  91.3 0.7 copy-start
  97.5 16.0 %all-to-all-start.2 = ((f32[32,1,960]{2,1,0:T(1,128)}), f32[32,1,960]{2,1,0:T(1,128)S(1)}, u32[]{:S(2)}, u32[]{:S(2)}) async-start(f32[32,1,960]{2,1,0:T(1,128)} %reshape.61), calls=%async_computation.2 | async-start | bytes 262144 | tf_op jit(solution)/shard_map/all_to_all | solution.py:46
  194.9 29.0 %all-to-all-start.3 = ((f32[16,1,768]{2,1,0:T(1,128)}), f32[16,1,768]{2,1,0:T(1,128)S(1)}, u32[]{:S(2)}, u32[]{:S(2)}) async-start(f32[16,1,768]{2,1,0:T(1,128)} %reshape.63), calls=%async_computation.3 | async-start | bytes 98304 | tf_op jit(solution)/shard_map/all_to_all | solution.py:71
  224.8 0.7 copy-start.4
  224.9 0.7 copy-start.5
